TPU v7x, 32 devices: a whole 2x2x4 slice. The times are simulated.
32 devices in a mesh: tm: 8 (over z, x), gauge: 4 (over y, core).
Axes of the slice: x: 2, y: 2, z: 4, core: 2. Of those that a mesh axis runs over, the one named last changes fastest.
Arguments:
- records: bfloat16 [65536, 1536], P('tm', 'gauge'), may hold values from -400 to 400
- offsets: int32 [64], P('tm'), may hold values from 0 to 960
- column_map: int32 [1536], replicated, may hold values from 0 to 1535, each once
- angles: float32 [512], replicated, may hold values from -3.140625 to 3.140625
Outputs:
- factor: float32 [1536, 1536], replicated
All inputs are finite; a program needn't handle non-finite values.
Results may differ from a plain program's by a relative error of at most 0.0014.
Values may be sent and summed in bfloat16 or wider, within the bound.
A program may use at most 128 MiB of HBM per device.

v0:
```python
import jax
import jax.numpy as jnp
from jax import lax
from jax.sharding import PartitionSpec as P

BLOCK = 1024
BAND = 64


def band_mask(offsets_here, total_rows):
    positions = jnp.arange(total_rows, dtype=jnp.int32)
    block_of = positions // BLOCK
    within = positions % BLOCK
    blocks = jnp.arange(offsets_here.shape[0], dtype=jnp.int32)
    inside = (
        (block_of[None, :] == blocks[:, None])
        & (within[None, :] >= offsets_here[:, None])
        & (within[None, :] < offsets_here[:, None] + BAND)
    )
    return inside.astype(jnp.bfloat16)


def drift_filter(rows, offsets_here):
    masks = band_mask(offsets_here, rows.shape[0])
    baseline = jnp.dot(masks, rows, preferred_element_type=jnp.float32) / BAND
    nblocks = offsets_here.shape[0]
    shaped = rows.astype(jnp.float32).reshape(nblocks, BLOCK, rows.shape[1]) - baseline[:, None, :]
    return shaped.reshape(rows.shape[0], rows.shape[1]).astype(jnp.bfloat16)


def rosette_rotate(full_rows, column_map, angles):
    count = angles.shape[0]
    picked = jnp.take(full_rows, column_map, axis=1)
    first_arm = picked[:, :count].astype(jnp.float32)
    middle_arm = picked[:, count : 2 * count].astype(jnp.float32)
    last_arm = picked[:, 2 * count :].astype(jnp.float32)
    shear = 2.0 * middle_arm - first_arm - last_arm
    cosine = jnp.cos(angles)[None, :]
    sine = jnp.sin(angles)[None, :]
    cos_sq = cosine * cosine
    sin_sq = sine * sine
    mixed = sine * cosine
    along_x = first_arm * cos_sq + last_arm * sin_sq + shear * mixed
    along_y = first_arm * sin_sq + last_arm * cos_sq - shear * mixed
    shear_new = 2.0 * (last_arm - first_arm) * mixed + shear * (cos_sq - sin_sq)
    return jnp.concatenate([along_x, along_y, shear_new], axis=1).astype(jnp.bfloat16)


def gram_of(rotated):
    return lax.dot_general(
        rotated, rotated, (((0,), (0,)), ((), ())), preferred_element_type=jnp.float32
    )


def shards(records, offsets, column_map, angles):
    filtered = drift_filter(records, offsets)
    regrouped = lax.all_to_all(filtered, "gauge", split_axis=0, concat_axis=1, tiled=True)
    rotated = rosette_rotate(regrouped, column_map, angles)
    total_rows = rotated.shape[0] * lax.axis_size("tm") * lax.axis_size("gauge")
    gram_full = lax.psum(gram_of(rotated), ("tm", "gauge"))
    return jnp.linalg.cholesky(gram_full / total_rows).T


def solution(mesh):
    placed = (P("tm", "gauge"), P("tm"), P(), P())
    return jax.shard_map(shards, mesh=mesh, in_specs=placed, out_specs=P(), check_vma=False)
```

profile of v0, /device:TPU:0, one launch (start us, length us, event | category | flops | bytes accessed | tf_op | source)
XLA Modules:
  0.0 719.3 jit_solution(9471501255185029127)
XLA Ops:
  7.4 3.9 convolution_multiply_fusion
  11.3 4.0 fusion
  15.3 8.7 %copy.5 = bf16[4,2048,384]{1,2,0:T(8,128)(2,1)} copy(bf16[4,2048,384]{2,1,0:T(8,128)(2,1)} %bitcast.75) | data formatting | bytes 12582912 | tf_op jit(solution)/shard_map/all_to_all | solution.py:57
  24.0 5.4 all-to-all-start
  29.5 71.2 %all-to-all-done = bf16[4,2048,384]{1,2,0:T(8,128)(2,1)} async-done(((bf16[4,2048,384]{1,2,0:T(8,128)(2,1)}), bf16[4,2048,384]{1,2,0:T(8,128)(2,1)}, u32[]{:S(2)}, u32[]{:S(2)}) %all-to-all-start) | async-done | bytes 6291488 | tf_op jit(solution)/shard_map/all_to_all | solution.py:57
  100.7 16.3 %gather_fusion = bf16[1536,2048]{1,0:T(8,128)(2,1)} fusion(bf16[2048,1536]{0,1:T(8,128)(2,1)} %bitcast.3, s32[2048]{0:T(1024)S(1)} %pad_clamp_fusion), kind=kCustom, calls=%fused_computation | custom fusion | bytes 12589056 | tf_op jit(solution)/shard_map/jit(_take)/gather | solution.py:33
  117.0 3.4 select_bitcast_fusion.1
  120.4 4.6 fusion.10
  125.0 17.2 %fusion.2 = f32[1536,1536]{0,1:T(8,128)} fusion(bf16[2048,512]{0,1:T(8,128)(2,1)} %get-tuple-element.9, bf16[2048,512]{0,1:T(8,128)(2,1)} %get-tuple-element.8, bf16[2048,512]{0,1:T(8,128)(2,1)S(1)} %get-tuple-element.7), kind=kOutput, calls=%fused_computation.14 | convolution fusion | flops 9682550784 | bytes 15728640 | tf_op jit(solution)/shard_map/dot_general | solution.py:50
  142.2 192.1 %all-reduce.3.cloned.1.call-done = f32[1536,1536]{0,1:T(8,128)} async-done(((f32[1536,1536]{0,1:T(8,128)}), f32[1536,1536]{0,1:T(8,128)}) %all-reduce.3.cloned.1.call-update) | async-done | bytes 9437200 | tf_op jit(solution)/shard_map/psum | solution.py:60
  334.3 8.5 %broadcast_multiply_fusion = f32[1536,1536]{0,1:T(8,128)} fusion(f32[1536,1536]{0,1:T(8,128)} %all-reduce.3.cloned.1.call-done), kind=kLoop, calls=%fused_computation.21 | loop fusion | flops 2359296 | bytes 18874368 | tf_op jit(solution)/shard_map/div | solution.py:61
  342.8 9.8 %copy.7 = f32[1536,1536]{1,0:T(8,128)} copy(f32[1536,1536]{0,1:T(8,128)} %broadcast_multiply_fusion) | data formatting | bytes 18874368 | tf_op jit(solution)/shard_map/div | solution.py:61
  352.6 12.4 %fusion.1 = f32[1536,1536]{1,0:T(8,128)} fusion(f32[1536,1536]{1,0:T(8,128)} %copy.7, f32[1536,1536]{0,1:T(8,128)} %all-reduce.3.cloned.1.call-done), kind=kLoop, calls=%fused_computation.4 | loop fusion | flops 7077888 | bytes 28311552 | tf_op jit(solution)/shard_map/jit(cholesky)/div | solution.py:61
  365.8 11.7 %cholesky.341 = f32[128,128]{1,0:T(8,128)S(1)} custom-call(f32[128,128]{1,0:T(8,128)S(1)} %cholesky.892), custom_call_target="Cholesky" | custom-call | tf_op jit(solution)/shard_map/jit(cholesky)/cholesky | solution.py:61
  378.3 9.8 %custom-call.91 = f32[1,128,128]{1,2,0:T(8,128)S(1)} custom-call(f32[1,128,128]{2,1,0:T(8,128)S(1)} %get-tuple-element.43), custom_call_target="InvertDiagBlocksLowerTriangular" | custom-call | tf_op jit(solution)/shard_map/jit(cholesky)/cholesky | solution.py:61
  388.1 4.8 cholesky.371
  392.9 2.8 constant_dynamic-update-slice_fusion.9
  397.6 12.1 %cholesky.362 = f32[128,128]{1,0:T(8,128)S(1)} custom-call(f32[128,128]{1,0:T(8,128)S(1)} %cholesky.896), custom_call_target="Cholesky" | custom-call | tf_op jit(solution)/shard_map/jit(cholesky)/cholesky | solution.py:61
  411.0 9.8 %custom-call.92 = f32[1,128,128]{1,2,0:T(8,128)S(1)} custom-call(f32[1,128,128]{2,1,0:T(8,128)S(1)} %get-tuple-element.40), custom_call_target="InvertDiagBlocksLowerTriangular" | custom-call | tf_op jit(solution)/shard_map/jit(cholesky)/cholesky | solution.py:61
  425.2 11.7 %cholesky.385 = f32[128,128]{1,0:T(8,128)S(1)} custom-call(f32[128,128]{1,0:T(8,128)S(1)} %cholesky.901), custom_call_target="Cholesky" | custom-call | tf_op jit(solution)/shard_map/jit(cholesky)/cholesky | solution.py:61
  438.3 10.0 %custom-call.93 = f32[1,128,128]{1,2,0:T(8,128)S(1)} custom-call(f32[1,128,128]{2,1,0:T(8,128)S(1)} %get-tuple-element.37), custom_call_target="InvertDiagBlocksLowerTriangular" | custom-call | tf_op jit(solution)/shard_map/jit(cholesky)/cholesky | solution.py:61
  449.7 3.3 convolution_subtract_fusion
  453.1 11.7 %cholesky.715 = f32[128,128]{1,0:T(8,128)S(1)} custom-call(f32[128,128]{1,0:T(8,128)S(1)} %cholesky.906), custom_call_target="Cholesky" | custom-call | tf_op jit(solution)/shard_map/jit(cholesky)/cholesky | solution.py:61
  466.1 9.8 %custom-call.94 = f32[1,128,128]{1,2,0:T(8,128)S(1)} custom-call(f32[1,128,128]{2,1,0:T(8,128)S(1)} %get-tuple-element.34), custom_call_target="InvertDiagBlocksLowerTriangular" | custom-call | tf_op jit(solution)/shard_map/jit(cholesky)/cholesky | solution.py:61
  477.4 3.6 fusion.34
  480.9 11.9 %cholesky.734 = f32[128,128]{1,0:T(8,128)S(1)} custom-call(f32[128,128]{1,0:T(8,128)S(1)} %cholesky.911), custom_call_target="Cholesky" | custom-call | tf_op jit(solution)/shard_map/jit(cholesky)/cholesky | solution.py:61
  494.2 9.8 %custom-call.95 = f32[1,128,128]{1,2,0:T(8,128)S(1)} custom-call(f32[1,128,128]{2,1,0:T(8,128)S(1)} %get-tuple-element.31), custom_call_target="InvertDiagBlocksLowerTriangular" | custom-call | tf_op jit(solution)/shard_map/jit(cholesky)/cholesky | solution.py:61
  505.3 3.8 fusion.37
  509.2 11.7 %cholesky.754 = f32[128,128]{1,0:T(8,128)S(1)} custom-call(f32[128,128]{1,0:T(8,128)S(1)} %cholesky.916), custom_call_target="Cholesky" | custom-call | tf_op jit(solution)/shard_map/jit(cholesky)/cholesky | solution.py:61
  522.2 10.2 %custom-call.96 = f32[1,128,128]{1,2,0:T(8,128)S(1)} custom-call(f32[1,128,128]{2,1,0:T(8,128)S(1)} %get-tuple-element.28), custom_call_target="InvertDiagBlocksLowerTriangular" | custom-call | tf_op jit(solution)/shard_map/jit(cholesky)/cholesky | solution.py:61
  533.7 3.9 fusion.40
  537.6 11.7 %cholesky.774 = f32[128,128]{1,0:T(8,128)S(1)} custom-call(f32[128,128]{1,0:T(8,128)S(1)} %cholesky.921), custom_call_target="Cholesky" | custom-call | tf_op jit(solution)/shard_map/jit(cholesky)/cholesky | solution.py:61
  550.6 9.8 %custom-call.97 = f32[1,128,128]{1,2,0:T(8,128)S(1)} custom-call(f32[1,128,128]{2,1,0:T(8,128)S(1)} %get-tuple-element.25), custom_call_target="InvertDiagBlocksLowerTriangular" | custom-call | tf_op jit(solution)/shard_map/jit(cholesky)/cholesky | solution.py:61
  561.6 4.0 fusion.43
  565.7 11.7 %cholesky.794 = f32[128,128]{1,0:T(8,128)S(1)} custom-call(f32[128,128]{1,0:T(8,128)S(1)} %cholesky.926), custom_call_target="Cholesky" | custom-call | tf_op jit(solution)/shard_map/jit(cholesky)/cholesky | solution.py:61
  578.8 9.8 %custom-call.98 = f32[1,128,128]{1,2,0:T(8,128)S(1)} custom-call(f32[1,128,128]{2,1,0:T(8,128)S(1)} %get-tuple-element.22), custom_call_target="InvertDiagBlocksLowerTriangular" | custom-call | tf_op jit(solution)/shard_map/jit(cholesky)/cholesky | solution.py:61
  589.7 3.6 fusion.46
  593.2 12.1 %cholesky.814 = f32[128,128]{1,0:T(8,128)S(1)} custom-call(f32[128,128]{1,0:T(8,128)S(1)} %cholesky.931), custom_call_target="Cholesky" | custom-call | tf_op jit(solution)/shard_map/jit(cholesky)/cholesky | solution.py:61
  606.7 9.8 %custom-call.99 = f32[1,128,128]{1,2,0:T(8,128)S(1)} custom-call(f32[1,128,128]{2,1,0:T(8,128)S(1)} %get-tuple-element.19), custom_call_target="InvertDiagBlocksLowerTriangular" | custom-call | tf_op jit(solution)/shard_map/jit(cholesky)/cholesky | solution.py:61
  617.6 3.3 fusion.49
  620.8 11.7 %cholesky.834 = f32[128,128]{1,0:T(8,128)S(1)} custom-call(f32[128,128]{1,0:T(8,128)S(1)} %cholesky.936), custom_call_target="Cholesky" | custom-call | tf_op jit(solution)/shard_map/jit(cholesky)/cholesky | solution.py:61
  633.9 9.8 %custom-call.100 = f32[1,128,128]{1,2,0:T(8,128)S(1)} custom-call(f32[1,128,128]{2,1,0:T(8,128)S(1)} %get-tuple-element.16), custom_call_target="InvertDiagBlocksLowerTriangular" | custom-call | tf_op jit(solution)/shard_map/jit(cholesky)/cholesky | solution.py:61
  644.6 2.9 fusion.52
  647.5 11.7 %cholesky.854 = f32[128,128]{1,0:T(8,128)S(1)} custom-call(f32[128,128]{1,0:T(8,128)S(1)} %cholesky.941), custom_call_target="Cholesky" | custom-call | tf_op jit(solution)/shard_map/jit(cholesky)/cholesky | solution.py:61
  660.5 9.8 %custom-call.101 = f32[1,128,128]{1,2,0:T(8,128)S(1)} custom-call(f32[1,128,128]{2,1,0:T(8,128)S(1)} %get-tuple-element.13), custom_call_target="InvertDiagBlocksLowerTriangular" | custom-call | tf_op jit(solution)/shard_map/jit(cholesky)/cholesky | solution.py:61
  673.5 11.7 %cholesky.872 = f32[128,128]{1,0:T(8,128)S(1)} custom-call(f32[128,128]{1,0:T(8,128)S(1)} %convolution_subtract_fusion.3), custom_call_target="Cholesky" | custom-call | tf_op jit(solution)/shard_map/jit(cholesky)/cholesky | solution.py:61
  694.2 8.5 %select_bitcast_fusion = f32[1536,1536]{0,1:T(8,128)} fusion(f32[1536,1536]{1,0:T(8,128)} %get-tuple-element.11, pred[]{:T(512)S(6)} %cholesky.891), kind=kLoop, calls=%fused_computation.5 | loop fusion | flops 7077888 | bytes 18874368 | tf_op jit(solution)/shard_map/transpose | solution.py:61
  702.7 9.6 %copy.8 = f32[1536,1536]{1,0:T(8,128)} copy(f32[1536,1536]{0,1:T(8,128)} %select_bitcast_fusion) | data formatting | bytes 18874368 | tf_op jit(solution)/shard_map/transpose | solution.py:61
  (63 shorter events, 36.4 us)
Async XLA Ops:
  6.5 4.7 copy-start
  15.3 14.1 %copy-start.1 = (s32[1536]{0:T(1024)S(1)}, s32[1536]{0:T(1024)}, u32[]{:S(2)}) copy-start(s32[1536]{0:T(1024)} %param.6) | copy-start | bytes 18436
  24.0 5.5 copy-start.2
  24.0 76.7 %all-to-all-start = ((bf16[4,2048,384]{1,2,0:T(8,128)(2,1)}), bf16[4,2048,384]{1,2,0:T(8,128)(2,1)}, u32[]{:S(2)}, u32[]{:S(2)}) async-start(bf16[4,2048,384]{1,2,0:T(8,128)(2,1)} %copy.5), calls=%async_computation | async-start | bytes 12582912 | tf_op jit(solution)/shard_map/all_to_all | solution.py:57
  29.3 305.0 %all-reduce.3.cloned.1.call-start = ((), (), s32[]{:S(2)}) async-start(), calls=%async_computation.1 | async-start | bytes 18874368 | tf_op jit(solution)/shard_map/psum | solution.py:60
Sparse Core Ops, SparseCore 0:
  142.3 191.9 all-reduce.2
where the time goes:
time: 727 us; the launch traced here: 719 us
  other arithmetic  308 us (42%)
  waiting for transfers between devices  263 us (36%)
  matrix products  71.4 us (10%)
  local copies, waits for them, and re-layouts  50.1 us (7%)
  between operations  21.6 us (3%)
    another operation x47, other arithmetic, shards(): return jnp.linalg.cholesky(gram_full / total_rows).T  265 us
    psum x1, waiting for transfers between devices, shards(): gram_full = lax.psum(gram_of(rotated), ('tm', 'gauge'))  192 us
    all_to_all x1, waiting for transfers between devices, shards(): lax.all_to_all(filtered, 'gauge', split_axis=0, concat_axis=1, tiled=True)  71.2 us
    another operation x22, matrix products, shards(): return jnp.linalg.cholesky(gram_full / total_rows).T  50.3 us
    div x2, other arithmetic, shards(): return jnp.linalg.cholesky(gram_full / total_rows).T  20.9 us
    dot_general x1, matrix products, gram_of(): lax.dot_general(rotated, rotated, (((0,), (0,)), ((), ())), preferred_ele...  17.2 us
    gather x1, local copies, waits for them, and re-layouts, rosette_rotate(): picked = jnp.take(full_rows, column_map, axis=1)  16.3 us
  transfers between devices with their start and end apart: 2, of which 2 were waited for; matrix products, arithmetic and copies ran while one was open for 0% of the time, Pallas kernels for 0%

commit v1 on v0

--- a/solution.py
+++ b/solution.py
@@ -1,6 +1,10 @@
+import functools
+
 import jax
 import jax.numpy as jnp
 from jax import lax
+from jax.experimental import pallas as pl
+from jax.experimental.pallas import tpu as pltpu
 from jax.sharding import PartitionSpec as P
 
 BLOCK = 1024
@@ -46,10 +50,144 @@
     return jnp.concatenate([along_x, along_y, shear_new], axis=1).astype(jnp.bfloat16)
 
 
-def gram_of(rotated):
-    return lax.dot_general(
-        rotated, rotated, (((0,), (0,)), ((), ())), preferred_element_type=jnp.float32
-    )
+N = 1536
+NB = 128
+TB = 384
+
+
+def factor_tile(state):
+    lane = lax.broadcasted_iota(jnp.int32, (8, NB), 1)
+    sub = lax.broadcasted_iota(jnp.int32, (8, NB), 0)
+    upper, inverse = [], []
+    for s in range(NB // 8):
+        base = 8 * s
+        rows = state[s]
+        here = (lane >= base) & (lane < base + 8)
+        cols = [jnp.broadcast_to(rows[:, base + k : base + k + 1], (8, NB)) for k in range(8)]
+        fwd = rows
+        merged = jnp.where(here, (lane - base == sub).astype(jnp.float32), rows)
+        fwd_inv = merged
+        jordan = merged
+        pivots = cols[0]
+        for j in range(8):
+            pivot = jnp.broadcast_to(cols[j][j : j + 1, :], (8, NB))
+            pivots = jnp.where(sub == j, pivot, pivots)
+            scaled = cols[j] * (1.0 / pivot)
+            both = jnp.where(sub == j, 0.0, scaled)
+            for k in range(j + 1, 8):
+                cols[k] = cols[k] - both * jnp.broadcast_to(cols[k][j : j + 1, :], (8, NB))
+            below = jnp.where(sub > j, scaled, 0.0)
+            fwd = fwd - below * jnp.broadcast_to(fwd[j : j + 1, :], (8, NB))
+            fwd_inv = fwd_inv - below * jnp.broadcast_to(fwd_inv[j : j + 1, :], (8, NB))
+            jordan = jordan - both * jnp.broadcast_to(jordan[j : j + 1, :], (8, NB))
+        root = lax.rsqrt(pivots)
+        root = root * (1.5 - 0.5 * pivots * root * root)
+        upper.append(jnp.where(lane >= sub + base, fwd * root, 0.0))
+        inverse.append(jnp.where(lane <= sub + base, fwd_inv * root, 0.0))
+        solved = jordan * (root * root)
+        solved_rows = [jnp.broadcast_to(solved[k : k + 1, :], (8, NB)) for k in range(8)]
+        for r in range(s + 1, NB // 8):
+            old = state[r]
+            new = jnp.where(here, 0.0, old)
+            for k in range(8):
+                new = new - jnp.broadcast_to(old[:, base + k : base + k + 1], (8, NB)) * solved_rows[k]
+            state[r] = new
+    return upper, inverse
+
+
+def cholesky_kernel(scale, *refs):
+    strips = refs[: N // TB]
+    a_ref, inv_ref, left_ref, right_ref = refs[N // TB :]
+    for i, strip in enumerate(strips):
+        a_ref[i * TB : (i + 1) * TB, i * TB :] = strip[...] * scale
+        if i > 0:
+            a_ref[i * TB : (i + 1) * TB, : i * TB] = jnp.zeros((TB, i * TB), jnp.float32)
+
+    def panel(k, carry):
+        top = pl.multiple_of(k * NB, NB)
+        rows = pl.ds(top, NB)
+        state = [a_ref[pl.ds(top + 8 * s, 8), pl.ds(top, NB)] for s in range(NB // 8)]
+        upper, inverse = factor_tile(state)
+        for s in range(NB // 8):
+            inv_ref[8 * s : 8 * s + 8, :] = inverse[s]
+        solved = jnp.dot(
+            inv_ref[...], a_ref[rows, :], precision=lax.Precision.HIGHEST, preferred_element_type=jnp.float32
+        )
+        col = lax.broadcasted_iota(jnp.int32, (NB, N), 1)
+        solved = jnp.where(col >= top + NB, solved, 0.0)
+        a_ref[rows, :] = solved
+        for s in range(NB // 8):
+            a_ref[pl.ds(top + 8 * s, 8), pl.ds(top, NB)] = upper[s]
+        high = solved.astype(jnp.bfloat16)
+        low = (solved - high.astype(jnp.float32)).astype(jnp.bfloat16)
+        right_ref[0:NB, :] = high
+        right_ref[NB : 2 * NB, :] = low
+        right_ref[2 * NB : 3 * NB, :] = high
+        right_ref[3 * NB : 4 * NB, :] = low
+        first = (k + 1) // (TB // NB)
+
+        def turn(i, carry):
+            at = pl.multiple_of(i * TB, TB)
+            turned = jnp.where(
+                lax.broadcasted_iota(jnp.int32, (NB, TB), 1) + at >= top + NB, a_ref[rows, pl.ds(at, TB)], 0.0
+            ).T
+            high = turned.astype(jnp.bfloat16)
+            low = (turned - high.astype(jnp.float32)).astype(jnp.bfloat16)
+            left_ref[pl.ds(at, TB), 0:NB] = high
+            left_ref[pl.ds(at, TB), NB : 2 * NB] = high
+            left_ref[pl.ds(at, TB), 2 * NB : 3 * NB] = low
+            left_ref[pl.ds(at, TB), 3 * NB : 4 * NB] = low
+            return carry
+
+        def update_row(i, carry):
+            at = pl.multiple_of(i * TB, TB)
+
+            def update(j, carry):
+                to = pl.multiple_of(j * TB, TB)
+                block = (pl.ds(at, TB), pl.ds(to, TB))
+                a_ref[block] -= jnp.dot(
+                    left_ref[pl.ds(at, TB), :], right_ref[:, pl.ds(to, TB)], preferred_element_type=jnp.float32
+                )
+                return carry
+
+            return lax.fori_loop(i, N // TB, update, carry)
+
+        @pl.when(k < N // NB - 1)
+        def _():
+            lax.fori_loop(first, N // TB, turn, 0)
+            lax.fori_loop(first, N // TB, update_row, 0)
+
+        return carry
+
+    lax.fori_loop(0, N // NB, panel, 0)
+
+
+def factor_of(strips, scale):
+    return pl.pallas_call(
+        functools.partial(cholesky_kernel, scale),
+        out_shape=jax.ShapeDtypeStruct((N, N), jnp.float32),
+        in_specs=[pl.BlockSpec(memory_space=pltpu.VMEM)] * len(strips),
+        out_specs=pl.BlockSpec(memory_space=pltpu.VMEM),
+        scratch_shapes=[
+            pltpu.VMEM((NB, NB), jnp.float32),
+            pltpu.VMEM((N, 4 * NB), jnp.bfloat16),
+            pltpu.VMEM((4 * NB, N), jnp.bfloat16),
+        ],
+        compiler_params=pltpu.CompilerParams(vmem_limit_bytes=48 * 1024 * 1024),
+        cost_estimate=pl.CostEstimate(flops=8 * N * N * N // 3, bytes_accessed=8 * N * N, transcendentals=0),
+    )(*strips)
+
+
+def gram_strips(rotated):
+    return [
+        lax.dot_general(
+            rotated[:, at : at + TB],
+            rotated[:, at:],
+            (((0,), (0,)), ((), ())),
+            preferred_element_type=jnp.float32,
+        )
+        for at in range(0, N, TB)
+    ]
 
 
 def shards(records, offsets, column_map, angles):
@@ -57,8 +195,8 @@
     regrouped = lax.all_to_all(filtered, "gauge", split_axis=0, concat_axis=1, tiled=True)
     rotated = rosette_rotate(regrouped, column_map, angles)
     total_rows = rotated.shape[0] * lax.axis_size("tm") * lax.axis_size("gauge")
-    gram_full = lax.psum(gram_of(rotated), ("tm", "gauge"))
-    return jnp.linalg.cholesky(gram_full / total_rows).T
+    strips = [lax.psum(strip, ("tm", "gauge")) for strip in gram_strips(rotated)]
+    return factor_of(strips, 1.0 / total_rows)
 
 
 def solution(mesh):

time: 727 us -> 395 us (0.54)
  other arithmetic: 308 us -> 11.6 us
  Pallas kernels: 0 us -> 91.6 us
  matrix products: 71.4 us -> 15.7 us
  waiting for transfers between devices: 263 us -> 226 us
  local copies, waits for them, and re-layouts: 50.1 us -> 30.4 us
  between operations: 21.6 us -> 13.5 us
    another operation x48 -> x1, other arithmetic: 270 us -> 3.28 us  [the longest x47 265 us: shards(): return jnp.linalg.cholesky(gram_full / total_rows).T]
    pallas_call x0 -> x1, Pallas kernels: none -> 91.6 us  [factor_of(): pl.pallas_call(functools.partial(cholesky_kernel, scale), out_shape=jax.S...]
    another operation x22 -> x0, matrix products: 50.3 us -> none  [shards(): return jnp.linalg.cholesky(gram_full / total_rows).T]
    psum x1, waiting for transfers between devices: 192 us -> 155 us  [shards(): lax.psum(strip, ('tm', 'gauge'))]
    div x2 -> x0, other arithmetic: 20.9 us -> none  [shards(): return jnp.linalg.cholesky(gram_full / total_rows).T]
    div x1 -> x0, local copies, waits for them, and re-layouts: 9.79 us -> none  [shards(): return jnp.linalg.cholesky(gram_full / total_rows).T]
    transpose x1 -> x0, local copies, waits for them, and re-layouts: 9.58 us -> none  [shards(): return jnp.linalg.cholesky(gram_full / total_rows).T]
    transpose x1 -> x0, other arithmetic: 8.5 us -> none  [shards(): return jnp.linalg.cholesky(gram_full / total_rows).T]
where the time goes in v1:
time: 395 us; the launch traced here: 394 us
  waiting for transfers between devices  226 us (57%)
  Pallas kernels  91.6 us (23%)
  local copies, waits for them, and re-layouts  30.4 us (8%)
  matrix products  15.7 us (4%)
  between operations  13.5 us (3%)
  other arithmetic  11.6 us (3%)
  starting transfers between devices  5.6 us (1%)
    psum x1, waiting for transfers between devices, shards(): lax.psum(strip, ('tm', 'gauge'))  155 us
    pallas_call x1, Pallas kernels, factor_of(): pl.pallas_call(functools.partial(cholesky_kernel, scale), out_shape=jax.S...  91.6 us
    all_to_all x1, waiting for transfers between devices, shards(): lax.all_to_all(filtered, 'gauge', split_axis=0, concat_axis=1, tiled=True)  71 us
    gather x1, local copies, waits for them, and re-layouts, rosette_rotate(): picked = jnp.take(full_rows, column_map, axis=1)  16.3 us
    dot_general x4, matrix products, gram_strips(): lax.dot_general(rotated[:, at:at + TB], rotated[:, at:], (((0,), (0,)), (...  11.8 us
    all_to_all x1, local copies, waits for them, and re-layouts, shards(): lax.all_to_all(filtered, 'gauge', split_axis=0, concat_axis=1, tiled=True)  8.64 us
  transfers between devices with their start and end apart: 2, of which 2 were waited for; matrix products, arithmetic and copies ran while one was open for 0% of the time, Pallas kernels for 0%

profile of v1, /device:TPU:0, one launch (start us, length us, event | category | flops | bytes accessed | tf_op | source)
XLA Modules:
  0.0 394.4 jit_solution(7326207746079342864)
XLA Ops:
  6.5 0.0 copy-start.4
  6.5 0.8 broadcast_add_fusion
  7.4 3.9 convolution_multiply_fusion
  11.3 0.0 copy-done.4
  11.3 4.0 %fusion = bf16[8192,384]{1,0:T(8,128)(2,1)} fusion(bf16[8192,384]{1,0:T(8,128)(2,1)S(1)} %copy-done.4, f32[8,384]{1,0:T(8,128)S(1)} %convolution_multiply_fusion), kind=kLoop, calls=%fused_computation.2 | loop fusion | flops 9437184 | bytes 12595200 | tf_op jit(solution)/shard_map/convert_element_type | solution.py:32
  15.3 8.6 %copy.5 = bf16[4,2048,384]{1,2,0:T(8,128)(2,1)} copy(bf16[4,2048,384]{2,1,0:T(8,128)(2,1)} %bitcast.11) | data formatting | bytes 12582912 | tf_op jit(solution)/shard_map/all_to_all | solution.py:195
  23.9 0.0 copy-start.5
  23.9 0.0 copy-start.6
  23.9 5.4 %all-to-all-start = ((bf16[4,2048,384]{1,2,0:T(8,128)(2,1)}), bf16[4,2048,384]{1,2,0:T(8,128)(2,1)}, u32[]{:S(2)}, u32[]{:S(2)}) async-start(bf16[4,2048,384]{1,2,0:T(8,128)(2,1)} %copy.5), calls=%async_computation | async-start | bytes 12582912 | tf_op jit(solution)/shard_map/all_to_all | solution.py:195
  29.3 0.2 all-reduce.3.cloned.1.call-start
  29.6 0.0 copy-done.5
  29.6 0.0 copy-done.6
  29.7 71.0 %all-to-all-done = bf16[4,2048,384]{1,2,0:T(8,128)(2,1)} async-done(((bf16[4,2048,384]{1,2,0:T(8,128)(2,1)}), bf16[4,2048,384]{1,2,0:T(8,128)(2,1)}, u32[]{:S(2)}, u32[]{:S(2)}) %all-to-all-start) | async-done | bytes 6291488 | tf_op jit(solution)/shard_map/all_to_all | solution.py:195
  100.7 16.3 %gather_fusion = bf16[1536,2048]{1,0:T(8,128)(2,1)} fusion(bf16[2048,1536]{0,1:T(8,128)(2,1)} %bitcast.3, s32[2048]{0:T(1024)S(1)} %pad_clamp_fusion), kind=kCustom, calls=%fused_computation | custom fusion | bytes 12589056 | tf_op jit(solution)/shard_map/jit(_take)/gather | solution.py:37
  117.0 3.4 select_bitcast_fusion
  120.4 3.3 fusion.15
  123.7 1.9 fusion.25
  125.5 2.5 fusion.23
  128.0 3.5 fusion.7
  131.5 4.0 %fusion.1 = f32[384,1536]{1,0:T(8,128)} fusion(bf16[2048,512]{0,1:T(8,128)(2,1)S(1)} %get-tuple-element.13, bf16[2048,512]{0,1:T(8,128)(2,1)S(1)} %get-tuple-element.12, bf16[2048,512]{0,1:T(8,128)(2,1)S(1)} %get-tuple-element.11), kind=kOutput, calls=%fused_computation.10 | convolution fusion | flops 2434793472 | bytes 10223616 | tf_op jit(solution)/shard_map/dot_general | solution.py:183
  135.5 0.0 all-reduce.3.cloned.1.call-update
  135.6 154.9 %all-reduce.3.cloned.1.call-done = (f32[384,1536]{1,0:T(8,128)}, f32[384,1152]{1,0:T(8,128)}, f32[384,768]{1,0:T(8,128)}, f32[384,384]{1,0:T(8,128)}) async-done(((f32[384,1536]{1,0:T(8,128)}, f32[384,1152]{1,0:T(8,128)}, f32[384,768]{1,0:T(8,128)}, f32[384,384]{1,0:T(8,128)}), (f32[384,1536]{1,0:T(8,128)}, f32[384,1152]{1,0:T(8,128)}, f32[384,768]{1,0:T(8,128)}, ...) | async-done | bytes 5898256 | tf_op jit(solution)/shard_map/psum | solution.py:198
  290.5 0.0 copy-start
  290.5 1.7 copy-done
  292.1 0.0 copy-start.1
  292.1 1.5 copy-done.1
  293.6 0.0 copy-start.2
  293.6 1.3 copy-done.2
  294.9 0.0 copy-start.3
  294.9 1.1 copy-done.3
  295.9 91.6 %shard_map.46 = f32[1536,1536]{1,0:T(8,128)} custom-call(f32[384,1536]{1,0:T(8,128)S(1)} %copy-done, f32[384,1152]{1,0:T(8,128)S(1)} %copy-done.1, f32[384,768]{1,0:T(8,128)S(1)} %copy-done.2, f32[384,384]{1,0:T(8,128)S(1)} %copy-done.3), custom_call_target="tpu_custom_call" | custom-call | flops 9663676416 | bytes 18874368 | tf_op jit(solution)/shard_map/pallas_call | solution.py:166
  (6 shorter events, 0.1 us)
Async XLA Ops:
  6.5 4.7 %copy-start.4 = (bf16[8192,384]{1,0:T(8,128)(2,1)S(1)}, bf16[8192,384]{1,0:T(8,128)(2,1)}, u32[]{:S(2)}) copy-start(bf16[8192,384]{1,0:T(8,128)(2,1)} %param.4) | copy-start | bytes 18874372
  23.9 5.6 %copy-start.5 = (s32[1536]{0:T(1024)S(1)}, s32[1536]{0:T(1024)}, u32[]{:S(2)}) copy-start(s32[1536]{0:T(1024)} %param.6) | copy-start | bytes 18436
  23.9 5.7 %copy-start.6 = (f32[512]{0:T(512)S(1)}, f32[512]{0:T(512)}, u32[]{:S(2)}) copy-start(f32[512]{0:T(512)} %param.7) | copy-start | bytes 6148
  23.9 76.7 %all-to-all-start = ((bf16[4,2048,384]{1,2,0:T(8,128)(2,1)}), bf16[4,2048,384]{1,2,0:T(8,128)(2,1)}, u32[]{:S(2)}, u32[]{:S(2)}) async-start(bf16[4,2048,384]{1,2,0:T(8,128)(2,1)} %copy.5), calls=%async_computation | async-start | bytes 12582912 | tf_op jit(solution)/shard_map/all_to_all | solution.py:195
  29.3 261.1 %all-reduce.3.cloned.1.call-start = ((), (), s32[]{:S(2)}) async-start(), calls=%async_computation.1 | async-start | bytes 11796480 | tf_op jit(solution)/shard_map/psum | solution.py:198
  290.5 1.7 copy-start
  292.1 1.5 copy-start.1
  293.6 1.3 copy-start.2
  294.9 1.1 copy-start.3
Sparse Core Ops, SparseCore 0:
  135.7 154.7 all-reduce.2

commit v2 on v1

--- a/solution.py
+++ b/solution.py
@@ -53,6 +53,166 @@
 N = 1536
 NB = 128
 TB = 384
+
+
+TILES = [(i, j) for i in range(N // NB) for j in range(i, N // NB)]
+MESH = pl.DeviceIdType.MESH
+
+
+def sum_kernel(sizes, *refs):
+    strips = refs[: N // TB]
+    out_ref, acc_ref, land_ref, rs_send, rs_recv, ag_send, ag_recv = refs[N // TB :]
+    size_z, size_x, size_y = sizes
+    tm, gauge = lax.axis_index("tm"), lax.axis_index("gauge")
+    at = {
+        "z": lax.div(tm, size_x),
+        "x": lax.rem(tm, size_x),
+        "y": lax.div(gauge, 2),
+        "core": lax.rem(gauge, 2),
+    }
+    size = {"z": size_z, "x": size_x, "y": size_y, "core": 2}
+
+    def peer(axis, d):
+        there = dict(at)
+        there[axis] = lax.rem(at[axis] + d, size[axis])
+        return there[axis], (there["z"] * size_x + there["x"], there["y"] * 2 + there["core"])
+
+    barrier = pltpu.get_barrier_semaphore()
+    friends = [peer(axis, d)[1] for axis in size for d in range(1, size[axis])]
+    for friend in friends:
+        pl.semaphore_signal(barrier, inc=1, device_id=friend, device_id_type=MESH)
+
+    for t, (i, j) in enumerate(TILES):
+        s = i * NB // TB
+        acc_ref[t * NB : (t + 1) * NB, :] = strips[s][
+            i * NB - s * TB : (i + 1) * NB - s * TB, j * NB - s * TB : (j + 1) * NB - s * TB
+        ]
+    total = acc_ref.shape[0]
+    filled = len(TILES) * NB
+    if filled < total:
+        acc_ref[filled:, :] = jnp.zeros((total - filled, NB), jnp.float32)
+
+    pl.semaphore_wait(barrier, len(friends))
+
+    orders = [("core", "y", "x", "z"), ("core", "x", "y", "z")]
+    base = [p * (total // 2) for p in range(2)]
+    length = [total // 2] * 2
+    slots = [0, 0]
+    marks = [[], []]
+
+    def scatter_start(p, stage):
+        axis = orders[p][stage]
+        n = size[axis]
+        piece = length[p] // n
+        copies = []
+        for d in range(1, n):
+            index, device = peer(axis, d)
+            slot = slots[p]
+            slots[p] += 1
+            land = land_ref.at[p, pl.ds(lands[p], piece), :]
+            copy = pltpu.make_async_remote_copy(
+                src_ref=acc_ref.at[pl.ds(pl.multiple_of(base[p] + index * piece, 8), piece), :],
+                dst_ref=land,
+                send_sem=rs_send.at[p, slot],
+                recv_sem=rs_recv.at[p, slot],
+                device_id=device,
+                device_id_type=MESH,
+            )
+            copy.start()
+            copies.append((copy, lands[p]))
+            lands[p] += piece
+        return copies, piece, axis
+
+    def scatter_finish(p, started):
+        copies, piece, axis = started
+        marks[p].append((base[p], length[p], axis))
+        base[p] = pl.multiple_of(base[p] + at[axis] * piece, 8)
+        length[p] = piece
+        rows = pl.ds(base[p], piece)
+        value = acc_ref[rows, :]
+        for copy, where in copies:
+            copy.wait_recv()
+            value = value + land_ref[p, where : where + piece, :]
+        if len(marks[p]) < 4:
+            acc_ref[rows, :] = value
+        else:
+            out_ref[rows, :] = value
+        sent.extend(copy for copy, where in copies)
+
+    def gather_start(p):
+        whole_base, whole_length, axis = marks[p][-1]
+        rows = pl.ds(base[p], length[p])
+        copies = []
+        for d in range(1, size[axis]):
+            index, device = peer(axis, d)
+            slot = slots[p]
+            slots[p] += 1
+            copy = pltpu.make_async_remote_copy(
+                src_ref=out_ref.at[rows, :],
+                dst_ref=out_ref.at[rows, :],
+                send_sem=ag_send.at[p, slot],
+                recv_sem=ag_recv.at[p, slot],
+                device_id=device,
+                device_id_type=MESH,
+            )
+            copy.start()
+            copies.append(copy)
+        return copies
+
+    def gather_finish(p, copies):
+        for copy in copies:
+            copy.wait_recv()
+        sent.extend(copies)
+        base[p], length[p], axis = marks[p].pop()
+
+    sent = []
+    lands = [0, 0]
+    flying = [scatter_start(p, 0) for p in range(2)]
+    for stage in range(4):
+        for p in range(2):
+            scatter_finish(p, flying[p])
+            if stage < 3:
+                flying[p] = scatter_start(p, stage + 1)
+            else:
+                slots[p] = 0
+                flying[p] = gather_start(p)
+    for stage in range(4):
+        for p in range(2):
+            gather_finish(p, flying[p])
+            if stage < 3:
+                flying[p] = gather_start(p)
+    for copy in sent:
+        copy.wait_send()
+
+
+def summed(strips, sizes):
+    size_z, size_x, size_y = sizes
+    unit = 4 * 8 * size_z * size_x * size_y
+    total = -(-len(TILES) * NB // unit) * unit
+    sends = size_z + size_x + size_y - 2
+    length = total // 2
+    landing = 0
+    for n in (2, size_x, size_y, size_z):
+        landing += length // n * (n - 1)
+        length //= n
+    return pl.pallas_call(
+        functools.partial(sum_kernel, sizes),
+        out_shape=jax.ShapeDtypeStruct((total, NB), jnp.float32),
+        in_specs=[pl.BlockSpec(memory_space=pltpu.VMEM)] * len(strips),
+        out_specs=pl.BlockSpec(memory_space=pltpu.VMEM),
+        scratch_shapes=[
+            pltpu.VMEM((total, NB), jnp.float32),
+            pltpu.VMEM((2, landing, NB), jnp.float32),
+            pltpu.SemaphoreType.DMA((2, sends)),
+            pltpu.SemaphoreType.DMA((2, sends)),
+            pltpu.SemaphoreType.DMA((2, sends)),
+            pltpu.SemaphoreType.DMA((2, sends)),
+        ],
+        compiler_params=pltpu.CompilerParams(
+            collective_id=0, has_side_effects=True, vmem_limit_bytes=48 * 1024 * 1024
+        ),
+        cost_estimate=pl.CostEstimate(flops=total * NB, bytes_accessed=16 * total * NB, transcendentals=0),
+    )(*strips)
 
 
 def factor_tile(state):
@@ -96,12 +256,10 @@
 
 
 def cholesky_kernel(scale, *refs):
-    strips = refs[: N // TB]
-    a_ref, inv_ref, left_ref, right_ref = refs[N // TB :]
-    for i, strip in enumerate(strips):
-        a_ref[i * TB : (i + 1) * TB, i * TB :] = strip[...] * scale
-        if i > 0:
-            a_ref[i * TB : (i + 1) * TB, : i * TB] = jnp.zeros((TB, i * TB), jnp.float32)
+    packed_ref, a_ref, inv_ref, left_ref, right_ref = refs
+    a_ref[...] = jnp.zeros_like(a_ref)
+    for t, (i, j) in enumerate(TILES):
+        a_ref[i * NB : (i + 1) * NB, j * NB : (j + 1) * NB] = packed_ref[t * NB : (t + 1) * NB, :] * scale
 
     def panel(k, carry):
         top = pl.multiple_of(k * NB, NB)
@@ -162,11 +320,11 @@
     lax.fori_loop(0, N // NB, panel, 0)
 
 
-def factor_of(strips, scale):
+def factor_of(packed, scale):
     return pl.pallas_call(
         functools.partial(cholesky_kernel, scale),
         out_shape=jax.ShapeDtypeStruct((N, N), jnp.float32),
-        in_specs=[pl.BlockSpec(memory_space=pltpu.VMEM)] * len(strips),
+        in_specs=[pl.BlockSpec(memory_space=pltpu.VMEM)],
         out_specs=pl.BlockSpec(memory_space=pltpu.VMEM),
         scratch_shapes=[
             pltpu.VMEM((NB, NB), jnp.float32),
@@ -175,7 +333,7 @@
         ],
         compiler_params=pltpu.CompilerParams(vmem_limit_bytes=48 * 1024 * 1024),
         cost_estimate=pl.CostEstimate(flops=8 * N * N * N // 3, bytes_accessed=8 * N * N, transcendentals=0),
-    )(*strips)
+    )(packed)
 
 
 def gram_strips(rotated):
@@ -190,13 +348,25 @@
     ]
 
 
+PARTS = 2
+
+
 def shards(records, offsets, column_map, angles):
-    filtered = drift_filter(records, offsets)
-    regrouped = lax.all_to_all(filtered, "gauge", split_axis=0, concat_axis=1, tiled=True)
-    rotated = rosette_rotate(regrouped, column_map, angles)
-    total_rows = rotated.shape[0] * lax.axis_size("tm") * lax.axis_size("gauge")
-    strips = [lax.psum(strip, ("tm", "gauge")) for strip in gram_strips(rotated)]
-    return factor_of(strips, 1.0 / total_rows)
+    total_rows = records.shape[0] * lax.axis_size("tm")
+    rows = records.shape[0] // PARTS
+    blocks = offsets.shape[0] // PARTS
+    strips = None
+    for part in range(PARTS):
+        filtered = drift_filter(
+            records[part * rows : (part + 1) * rows], offsets[part * blocks : (part + 1) * blocks]
+        )
+        regrouped = lax.all_to_all(filtered, "gauge", split_axis=0, concat_axis=1, tiled=True)
+        rotated = rosette_rotate(regrouped, column_map, angles)
+        terms = gram_strips(rotated)
+        strips = terms if strips is None else [one + other for one, other in zip(strips, terms)]
+    size_y = lax.axis_size("gauge") // 2
+    sizes = (lax.axis_size("tm") // size_y, size_y, size_y)
+    return factor_of(summed(strips, sizes), 1.0 / total_rows)
 
 
 def solution(mesh):

time: 395 us -> 303 us (0.77)
  waiting for transfers between devices: 226 us -> 63.3 us
  Pallas kernels: 91.6 us -> 182 us
  between operations: 13.5 us -> 0.16 us
  local copies, waits for them, and re-layouts: 30.4 us -> 26.2 us
    psum x1 -> x0, waiting for transfers between devices: 155 us -> none  [shards(): lax.psum(strip, ('tm', 'gauge'))]
    pallas_call x0 -> x1, Pallas kernels: none -> 90.3 us  [summed(): pl.pallas_call(functools.partial(sum_kernel, sizes), out_shape=jax.ShapeD...]
    all_to_all x1 -> x2, waiting for transfers between devices: 71 us -> 63.3 us  [shards(): lax.all_to_all(filtered, 'gauge', split_axis=0, concat_axis=1, tiled=True)]
    dot_general x4 -> x8, matrix products: 11.8 us -> 8.09 us  [gram_strips(): lax.dot_general(rotated[:, at:at + TB], rotated[:, at:], (((0,), (0,)), (...]
    all_to_all x1 -> x2, starting transfers between devices: 5.38 us -> 8.9 us  [shards(): lax.all_to_all(filtered, 'gauge', split_axis=0, concat_axis=1, tiled=True)]
    all_to_all x1 -> x2, local copies, waits for them, and re-layouts: 8.64 us -> 7.57 us  [shards(): lax.all_to_all(filtered, 'gauge', split_axis=0, concat_axis=1, tiled=True)]
    gather x1 -> x2, local copies, waits for them, and re-layouts: 16.3 us -> 16.1 us  [rosette_rotate(): picked = jnp.take(full_rows, column_map, axis=1)]
  transfers between devices with their start and end apart: 2 -> 2, of which waited for: 2 -> 2; matrix products, arithmetic and copies ran while one was open for 0% -> 4% of each run, Pallas kernels for 0% -> 0%
where the time goes in v2:
time: 303 us
  Pallas kernels  182 us (60%)
  waiting for transfers between devices  63.3 us (21%)
  local copies, waits for them, and re-layouts  26.2 us (9%)
  matrix products  13.3 us (4%)
  other arithmetic  9.18 us (3%)
  starting transfers between devices  8.9 us (3%)
    pallas_call x1, Pallas kernels, factor_of(): pl.pallas_call(functools.partial(cholesky_kernel, scale), out_shape=jax.S...  91.6 us
    pallas_call x1, Pallas kernels, summed(): pl.pallas_call(functools.partial(sum_kernel, sizes), out_shape=jax.ShapeD...  90.3 us
    all_to_all x2, waiting for transfers between devices, shards(): lax.all_to_all(filtered, 'gauge', split_axis=0, concat_axis=1, tiled=True)  63.3 us
    gather x2, local copies, waits for them, and re-layouts, rosette_rotate(): picked = jnp.take(full_rows, column_map, axis=1)  16.1 us
    all_to_all x2, starting transfers between devices, shards(): lax.all_to_all(filtered, 'gauge', split_axis=0, concat_axis=1, tiled=True)  8.9 us
    dot_general x8, matrix products, gram_strips(): lax.dot_general(rotated[:, at:at + TB], rotated[:, at:], (((0,), (0,)), (...  8.09 us
    all_to_all x2, local copies, waits for them, and re-layouts, shards(): lax.all_to_all(filtered, 'gauge', split_axis=0, concat_axis=1, tiled=True)  7.57 us
  transfers between devices with their start and end apart: 2, of which 2 were waited for; matrix products, arithmetic and copies ran while one was open for 4% of the time, Pallas kernels for 0%

profile of v2, /device:TPU:0, one launch (start us, length us, event | category | flops | bytes accessed | tf_op | source)
XLA Modules:
  0.0 302.9 jit_solution(17923354657015978239)
XLA Ops:
  0.0 0.8 fusion.108
  0.8 0.0 copy-start.2
  0.8 2.6 fusion.57
  3.4 2.6 fusion.60
  6.0 0.0 copy-done.2
  6.0 2.4 fusion
  8.4 2.9 copy.5
  11.3 4.2 %all-to-all-start = ((bf16[4,1024,384]{1,2,0:T(8,128)(2,1)}), bf16[4,1024,384]{1,2,0:T(8,128)(2,1)S(1)}, u32[]{:S(2)}, u32[]{:S(2)}) async-start(bf16[4,1024,384]{1,2,0:T(8,128)(2,1)} %copy.5), calls=%async_computation | async-start | bytes 6291456 | tf_op jit(solution)/shard_map/all_to_all | solution.py:363
  15.6 4.7 %copy.6 = bf16[4,1024,384]{1,2,0:T(8,128)(2,1)} copy(bf16[4,1024,384]{2,1,0:T(8,128)(2,1)} %bitcast.21) | data formatting | bytes 6291456 | tf_op jit(solution)/shard_map/all_to_all | solution.py:363
  20.2 0.0 copy-start.3
  20.2 0.0 copy-start.4
  20.2 32.3 %all-to-all-done = bf16[4,1024,384]{1,2,0:T(8,128)(2,1)S(1)} async-done(((bf16[4,1024,384]{1,2,0:T(8,128)(2,1)}), bf16[4,1024,384]{1,2,0:T(8,128)(2,1)S(1)}, u32[]{:S(2)}, u32[]{:S(2)}) %all-to-all-start) | async-done | bytes 3145760 | tf_op jit(solution)/shard_map/all_to_all | solution.py:363
  52.6 4.7 %all-to-all-start.1 = ((bf16[4,1024,384]{1,2,0:T(8,128)(2,1)}), bf16[4,1024,384]{1,2,0:T(8,128)(2,1)}, u32[]{:S(2)}, u32[]{:S(2)}) async-start(bf16[4,1024,384]{1,2,0:T(8,128)(2,1)} %copy.6), calls=%async_computation.1 | async-start | bytes 6291456 | tf_op jit(solution)/shard_map/all_to_all | solution.py:363
  57.3 0.0 copy-done.3
  57.3 0.0 copy-done.4
  57.4 5.9 %gather_fusion = bf16[1536,1024]{1,0:T(8,128)(2,1)} fusion(bf16[1024,1536]{0,1:T(8,128)(2,1)S(1)} %bitcast.20, s32[2048]{0:T(1024)S(1)} %pad_clamp_fusion), kind=kCustom, calls=%fused_computation.clone | custom fusion | bytes 6297600 | tf_op jit(solution)/shard_map/jit(_take)/gather | solution.py:37
  63.3 31.0 %all-to-all-done.1 = bf16[4,1024,384]{1,2,0:T(8,128)(2,1)} async-done(((bf16[4,1024,384]{1,2,0:T(8,128)(2,1)}), bf16[4,1024,384]{1,2,0:T(8,128)(2,1)}, u32[]{:S(2)}, u32[]{:S(2)}) %all-to-all-start.1) | async-done | bytes 3145760 | tf_op jit(solution)/shard_map/all_to_all | solution.py:363
  94.3 0.0 copy-start.1
  94.3 10.2 %gather_fusion.1 = bf16[1536,1024]{1,0:T(8,128)(2,1)} fusion(bf16[1024,1536]{0,1:T(8,128)(2,1)} %bitcast.8, s32[2048]{0:T(1024)S(1)} %pad_clamp_fusion), kind=kCustom, calls=%fused_computation.1.clone | custom fusion | bytes 6297600 | tf_op jit(solution)/shard_map/jit(_take)/gather | solution.py:37
  104.5 0.0 copy-done.1
  104.5 2.5 select_bitcast_fusion
  107.0 1.6 fusion.34
  108.6 0.6 fusion.64
  109.2 1.2 fusion.26
  110.4 1.4 fusion.2
  111.9 1.8 fusion.43
  113.7 0.6 convolution_add_fusion.1.refs_3_
  114.3 0.8 fusion.52
  115.1 0.8 fusion.56.refs_2_
  115.9 1.4 fusion.14.refs_0_
  117.3 1.2 convolution_add_fusion.refs_1_
  118.6 90.3 %shard_map.46.refs_0_ = f32[10240,128]{1,0:T(8,128)} custom-call(f32[384,1536]{1,0:T(8,128)S(1)} %fusion.14.refs_0_, f32[384,1152]{1,0:T(8,128)S(1)} %convolution_add_fusion.refs_1_, f32[384,768]{1,0:T(8,128)S(1)} %fusion.56.refs_2_, f32[384,384]{1,0:T(8,128)S(1)} %convolution_add_fusion.1.refs_3_), custom_call_target="tpu_custom_call" | custom-call | flops 1310720 | bytes 20971520 | tf_op jit(solution)/shard_map/pallas_call | solution.py:198
  208.8 0.0 copy-start
  208.9 2.5 copy-done
  211.3 91.6 %shard_map.47 = f32[1536,1536]{1,0:T(8,128)} custom-call(f32[10240,128]{1,0:T(8,128)S(1)} %copy-done), custom_call_target="tpu_custom_call" | custom-call | flops 9663676416 | bytes 18874368 | tf_op jit(solution)/shard_map/pallas_call | solution.py:324
  (6 shorter events, 0.1 us)
Async XLA Ops:
  0.8 5.2 %copy-start.2 = (bf16[8192,384]{1,0:T(8,128)(2,1)S(1)}, bf16[8192,384]{1,0:T(8,128)(2,1)}, u32[]{:S(2)}) copy-start(bf16[8192,384]{1,0:T(8,128)(2,1)} %param.6) | copy-start | bytes 18874372
  11.3 41.2 %all-to-all-start = ((bf16[4,1024,384]{1,2,0:T(8,128)(2,1)}), bf16[4,1024,384]{1,2,0:T(8,128)(2,1)S(1)}, u32[]{:S(2)}, u32[]{:S(2)}) async-start(bf16[4,1024,384]{1,2,0:T(8,128)(2,1)} %copy.5), calls=%async_computation | async-start | bytes 6291456 | tf_op jit(solution)/shard_map/all_to_all | solution.py:363
  20.2 37.0 %copy-start.3 = (s32[1536]{0:T(1024)S(1)}, s32[1536]{0:T(1024)}, u32[]{:S(2)}) copy-start(s32[1536]{0:T(1024)} %param.8) | copy-start | bytes 18436
  20.2 37.0 %copy-start.4 = (f32[512]{0:T(512)S(1)}, f32[512]{0:T(512)}, u32[]{:S(2)}) copy-start(f32[512]{0:T(512)} %param.9) | copy-start | bytes 6148
  52.6 41.7 %all-to-all-start.1 = ((bf16[4,1024,384]{1,2,0:T(8,128)(2,1)}), bf16[4,1024,384]{1,2,0:T(8,128)(2,1)}, u32[]{:S(2)}, u32[]{:S(2)}) async-start(bf16[4,1024,384]{1,2,0:T(8,128)(2,1)} %copy.6), calls=%async_computation.1 | async-start | bytes 6291456 | tf_op jit(solution)/shard_map/all_to_all | solution.py:363
  94.3 10.2 %copy-start.1 = (bf16[1536,1024]{1,0:T(8,128)(2,1)S(1)}, bf16[1536,1024]{1,0:T(8,128)(2,1)}, u32[]{:S(2)}) copy-start(bf16[1536,1024]{1,0:T(8,128)(2,1)} %gather_fusion) | copy-start | bytes 9437188
  208.8 2.5 copy-start

commit v3 on v2

--- a/solution.py
+++ b/solution.py
@@ -57,6 +57,7 @@
 
 TILES = [(i, j) for i in range(N // NB) for j in range(i, N // NB)]
 MESH = pl.DeviceIdType.MESH
+PIECES = 4
 
 
 def sum_kernel(sizes, *refs):
@@ -94,11 +95,11 @@
 
     pl.semaphore_wait(barrier, len(friends))
 
-    orders = [("core", "y", "x", "z"), ("core", "x", "y", "z")]
-    base = [p * (total // 2) for p in range(2)]
-    length = [total // 2] * 2
-    slots = [0, 0]
-    marks = [[], []]
+    orders = [("core", "y", "x", "z"), ("core", "x", "y", "z")] * (PIECES // 2)
+    base = [p * (total // PIECES) for p in range(PIECES)]
+    length = [total // PIECES] * PIECES
+    slots = [0] * PIECES
+    marks = [[] for p in range(PIECES)]
 
     def scatter_start(p, stage):
         axis = orders[p][stage]
@@ -166,10 +167,10 @@
         base[p], length[p], axis = marks[p].pop()
 
     sent = []
-    lands = [0, 0]
-    flying = [scatter_start(p, 0) for p in range(2)]
+    lands = [0] * PIECES
+    flying = [scatter_start(p, 0) for p in range(PIECES)]
     for stage in range(4):
-        for p in range(2):
+        for p in range(PIECES):
             scatter_finish(p, flying[p])
             if stage < 3:
                 flying[p] = scatter_start(p, stage + 1)
@@ -177,7 +178,7 @@
                 slots[p] = 0
                 flying[p] = gather_start(p)
     for stage in range(4):
-        for p in range(2):
+        for p in range(PIECES):
             gather_finish(p, flying[p])
             if stage < 3:
                 flying[p] = gather_start(p)
@@ -187,10 +188,10 @@
 
 def summed(strips, sizes):
     size_z, size_x, size_y = sizes
-    unit = 4 * 8 * size_z * size_x * size_y
+    unit = 2 * PIECES * 8 * size_z * size_x * size_y
     total = -(-len(TILES) * NB // unit) * unit
     sends = size_z + size_x + size_y - 2
-    length = total // 2
+    length = total // PIECES
     landing = 0
     for n in (2, size_x, size_y, size_z):
         landing += length // n * (n - 1)
@@ -202,11 +203,11 @@
         out_specs=pl.BlockSpec(memory_space=pltpu.VMEM),
         scratch_shapes=[
             pltpu.VMEM((total, NB), jnp.float32),
-            pltpu.VMEM((2, landing, NB), jnp.float32),
-            pltpu.SemaphoreType.DMA((2, sends)),
-            pltpu.SemaphoreType.DMA((2, sends)),
-            pltpu.SemaphoreType.DMA((2, sends)),
-            pltpu.SemaphoreType.DMA((2, sends)),
+            pltpu.VMEM((PIECES, landing, NB), jnp.float32),
+            pltpu.SemaphoreType.DMA((PIECES, sends)),
+            pltpu.SemaphoreType.DMA((PIECES, sends)),
+            pltpu.SemaphoreType.DMA((PIECES, sends)),
+            pltpu.SemaphoreType.DMA((PIECES, sends)),
         ],
         compiler_params=pltpu.CompilerParams(
             collective_id=0, has_side_effects=True, vmem_limit_bytes=48 * 1024 * 1024
@@ -229,11 +230,18 @@
         fwd_inv = merged
         jordan = merged
         pivots = cols[0]
+        pivot = jnp.broadcast_to(cols[0][0:1, :], (8, NB))
         for j in range(8):
-            pivot = jnp.broadcast_to(cols[j][j : j + 1, :], (8, NB))
             pivots = jnp.where(sub == j, pivot, pivots)
-            scaled = cols[j] * (1.0 / pivot)
-            both = jnp.where(sub == j, 0.0, scaled)
+            reciprocal = 1.0 / pivot
+            masked = jnp.where(sub == j, 0.0, cols[j])
+            scaled = cols[j] * reciprocal
+            both = masked * reciprocal
+            if j < 7:
+                corner = jnp.broadcast_to(cols[j + 1][j + 1 : j + 2, :], (8, NB))
+                across = jnp.broadcast_to(cols[j + 1][j : j + 1, :], (8, NB))
+                down = jnp.broadcast_to(cols[j][j + 1 : j + 2, :], (8, NB))
+                pivot = corner - (down * across) * reciprocal
             for k in range(j + 1, 8):
                 cols[k] = cols[k] - both * jnp.broadcast_to(cols[k][j : j + 1, :], (8, NB))
             below = jnp.where(sub > j, scaled, 0.0)
@@ -268,34 +276,33 @@
         upper, inverse = factor_tile(state)
         for s in range(NB // 8):
             inv_ref[8 * s : 8 * s + 8, :] = inverse[s]
-        solved = jnp.dot(
-            inv_ref[...], a_ref[rows, :], precision=lax.Precision.HIGHEST, preferred_element_type=jnp.float32
-        )
-        col = lax.broadcasted_iota(jnp.int32, (NB, N), 1)
-        solved = jnp.where(col >= top + NB, solved, 0.0)
-        a_ref[rows, :] = solved
+        def solve(i, carry):
+            at = pl.multiple_of(i * TB, TB)
+            part = pl.ds(at, TB)
+            solved = jnp.dot(
+                inv_ref[...], a_ref[rows, part], precision=lax.Precision.HIGHEST, preferred_element_type=jnp.float32
+            )
+            col = lax.broadcasted_iota(jnp.int32, (NB, TB), 1) + at
+            solved = jnp.where(col >= top + NB, solved, 0.0)
+            a_ref[rows, part] = solved
+            high = solved.astype(jnp.bfloat16)
+            low = (solved - high.astype(jnp.float32)).astype(jnp.bfloat16)
+            right_ref[0:NB, part] = high
+            right_ref[NB : 2 * NB, part] = low
+            right_ref[2 * NB : 3 * NB, part] = high
+            right_ref[3 * NB : 4 * NB, part] = low
+            turned = solved.T
+            high = turned.astype(jnp.bfloat16)
+            low = (turned - high.astype(jnp.float32)).astype(jnp.bfloat16)
+            left_ref[part, 0:NB] = high
+            left_ref[part, NB : 2 * NB] = high
+            left_ref[part, 2 * NB : 3 * NB] = low
+            left_ref[part, 3 * NB : 4 * NB] = low
+            return carry
+
+        lax.fori_loop(k // (TB // NB), N // TB, solve, 0)
         for s in range(NB // 8):
             a_ref[pl.ds(top + 8 * s, 8), pl.ds(top, NB)] = upper[s]
-        high = solved.astype(jnp.bfloat16)
-        low = (solved - high.astype(jnp.float32)).astype(jnp.bfloat16)
-        right_ref[0:NB, :] = high
-        right_ref[NB : 2 * NB, :] = low
-        right_ref[2 * NB : 3 * NB, :] = high
-        right_ref[3 * NB : 4 * NB, :] = low
-        first = (k + 1) // (TB // NB)
-
-        def turn(i, carry):
-            at = pl.multiple_of(i * TB, TB)
-            turned = jnp.where(
-                lax.broadcasted_iota(jnp.int32, (NB, TB), 1) + at >= top + NB, a_ref[rows, pl.ds(at, TB)], 0.0
-            ).T
-            high = turned.astype(jnp.bfloat16)
-            low = (turned - high.astype(jnp.float32)).astype(jnp.bfloat16)
-            left_ref[pl.ds(at, TB), 0:NB] = high
-            left_ref[pl.ds(at, TB), NB : 2 * NB] = high
-            left_ref[pl.ds(at, TB), 2 * NB : 3 * NB] = low
-            left_ref[pl.ds(at, TB), 3 * NB : 4 * NB] = low
-            return carry
 
         def update_row(i, carry):
             at = pl.multiple_of(i * TB, TB)
@@ -310,12 +317,7 @@
 
             return lax.fori_loop(i, N // TB, update, carry)
 
-        @pl.when(k < N // NB - 1)
-        def _():
-            lax.fori_loop(first, N // TB, turn, 0)
-            lax.fori_loop(first, N // TB, update_row, 0)
-
-        return carry
+        return lax.fori_loop((k + 1) // (TB // NB), N // TB, update_row, carry)
 
     lax.fori_loop(0, N // NB, panel, 0)
 

time: 303 us -> 287 us (0.947)
  Pallas kernels: 182 us -> 165 us
    pallas_call x1, Pallas kernels: 90.3 us -> 81 us  [summed(): pl.pallas_call(functools.partial(sum_kernel, sizes), out_shape=jax.ShapeD...]
    pallas_call x1, Pallas kernels: 91.6 us -> 84.2 us  [factor_of(): pl.pallas_call(functools.partial(cholesky_kernel, scale), out_shape=jax.S...]
where the time goes in v3:
time: 287 us; the launch traced here: 286 us
  Pallas kernels  165 us (57%)
  waiting for transfers between devices  63.3 us (22%)
  local copies, waits for them, and re-layouts  26.2 us (9%)
  matrix products  13.3 us (5%)
  other arithmetic  9.18 us (3%)
  starting transfers between devices  8.9 us (3%)
    pallas_call x1, Pallas kernels, factor_of(): pl.pallas_call(functools.partial(cholesky_kernel, scale), out_shape=jax.S...  84.2 us
    pallas_call x1, Pallas kernels, summed(): pl.pallas_call(functools.partial(sum_kernel, sizes), out_shape=jax.ShapeD...  81 us
    all_to_all x2, waiting for transfers between devices, shards(): lax.all_to_all(filtered, 'gauge', split_axis=0, concat_axis=1, tiled=True)  63.3 us
    gather x2, local copies, waits for them, and re-layouts, rosette_rotate(): picked = jnp.take(full_rows, column_map, axis=1)  16.1 us
    all_to_all x2, starting transfers between devices, shards(): lax.all_to_all(filtered, 'gauge', split_axis=0, concat_axis=1, tiled=True)  8.9 us
    dot_general x8, matrix products, gram_strips(): lax.dot_general(rotated[:, at:at + TB], rotated[:, at:], (((0,), (0,)), (...  8.09 us
    all_to_all x2, local copies, waits for them, and re-layouts, shards(): lax.all_to_all(filtered, 'gauge', split_axis=0, concat_axis=1, tiled=True)  7.57 us
  transfers between devices with their start and end apart: 2, of which 2 were waited for; matrix products, arithmetic and copies ran while one was open for 4% of the time, Pallas kernels for 0%

profile of v3, /device:TPU:0, one launch (start us, length us, event | category | flops | bytes accessed | tf_op | source)
XLA Modules:
  0.0 286.2 jit_solution(3879482644359540096)
XLA Ops:
  0.0 0.8 fusion.108
  0.8 0.0 copy-start.2
  0.8 2.6 fusion.57
  3.4 2.6 fusion.60
  6.0 0.0 copy-done.2
  6.0 2.4 fusion
  8.4 2.9 %copy.5 = bf16[4,1024,384]{1,2,0:T(8,128)(2,1)} copy(bf16[4,1024,384]{2,1,0:T(8,128)(2,1)S(1)} %bitcast.22) | data formatting | bytes 6291456 | tf_op jit(solution)/shard_map/all_to_all | solution.py:365
  11.3 4.2 %all-to-all-start = ((bf16[4,1024,384]{1,2,0:T(8,128)(2,1)}), bf16[4,1024,384]{1,2,0:T(8,128)(2,1)S(1)}, u32[]{:S(2)}, u32[]{:S(2)}) async-start(bf16[4,1024,384]{1,2,0:T(8,128)(2,1)} %copy.5), calls=%async_computation | async-start | bytes 6291456 | tf_op jit(solution)/shard_map/all_to_all | solution.py:365
  15.6 4.7 %copy.6 = bf16[4,1024,384]{1,2,0:T(8,128)(2,1)} copy(bf16[4,1024,384]{2,1,0:T(8,128)(2,1)} %bitcast.21) | data formatting | bytes 6291456 | tf_op jit(solution)/shard_map/all_to_all | solution.py:365
  20.2 0.0 copy-start.3
  20.2 0.0 copy-start.4
  20.2 32.3 %all-to-all-done = bf16[4,1024,384]{1,2,0:T(8,128)(2,1)S(1)} async-done(((bf16[4,1024,384]{1,2,0:T(8,128)(2,1)}), bf16[4,1024,384]{1,2,0:T(8,128)(2,1)S(1)}, u32[]{:S(2)}, u32[]{:S(2)}) %all-to-all-start) | async-done | bytes 3145760 | tf_op jit(solution)/shard_map/all_to_all | solution.py:365
  52.6 4.7 %all-to-all-start.1 = ((bf16[4,1024,384]{1,2,0:T(8,128)(2,1)}), bf16[4,1024,384]{1,2,0:T(8,128)(2,1)}, u32[]{:S(2)}, u32[]{:S(2)}) async-start(bf16[4,1024,384]{1,2,0:T(8,128)(2,1)} %copy.6), calls=%async_computation.1 | async-start | bytes 6291456 | tf_op jit(solution)/shard_map/all_to_all | solution.py:365
  57.3 0.0 copy-done.3
  57.3 0.0 copy-done.4
  57.4 5.9 %gather_fusion = bf16[1536,1024]{1,0:T(8,128)(2,1)} fusion(bf16[1024,1536]{0,1:T(8,128)(2,1)S(1)} %bitcast.20, s32[2048]{0:T(1024)S(1)} %pad_clamp_fusion), kind=kCustom, calls=%fused_computation.clone | custom fusion | bytes 6297600 | tf_op jit(solution)/shard_map/jit(_take)/gather | solution.py:37
  63.3 31.0 %all-to-all-done.1 = bf16[4,1024,384]{1,2,0:T(8,128)(2,1)} async-done(((bf16[4,1024,384]{1,2,0:T(8,128)(2,1)}), bf16[4,1024,384]{1,2,0:T(8,128)(2,1)}, u32[]{:S(2)}, u32[]{:S(2)}) %all-to-all-start.1) | async-done | bytes 3145760 | tf_op jit(solution)/shard_map/all_to_all | solution.py:365
  94.3 0.0 copy-start.1
  94.3 10.2 %gather_fusion.1 = bf16[1536,1024]{1,0:T(8,128)(2,1)} fusion(bf16[1024,1536]{0,1:T(8,128)(2,1)} %bitcast.8, s32[2048]{0:T(1024)S(1)} %pad_clamp_fusion), kind=kCustom, calls=%fused_computation.1.clone | custom fusion | bytes 6297600 | tf_op jit(solution)/shard_map/jit(_take)/gather | solution.py:37
  104.5 0.0 copy-done.1
  104.5 2.5 select_bitcast_fusion
  107.0 1.6 fusion.34
  108.6 0.6 fusion.64
  109.2 1.2 fusion.26
  110.4 1.4 fusion.2
  111.9 1.8 fusion.43
  113.7 0.6 convolution_add_fusion.1.refs_3_
  114.3 0.8 fusion.52
  115.1 0.8 fusion.56.refs_2_
  115.9 1.4 fusion.14.refs_0_
  117.3 1.2 convolution_add_fusion.refs_1_
  118.6 81.0 %shard_map.46.refs_0_ = f32[10240,128]{1,0:T(8,128)} custom-call(f32[384,1536]{1,0:T(8,128)S(1)} %fusion.14.refs_0_, f32[384,1152]{1,0:T(8,128)S(1)} %convolution_add_fusion.refs_1_, f32[384,768]{1,0:T(8,128)S(1)} %fusion.56.refs_2_, f32[384,384]{1,0:T(8,128)S(1)} %convolution_add_fusion.1.refs_3_), custom_call_target="tpu_custom_call" | custom-call | flops 1310720 | bytes 20971520 | tf_op jit(solution)/shard_map/pallas_call | solution.py:199
  199.6 0.0 copy-start
  199.6 2.5 copy-done
  202.0 84.2 %shard_map.47 = f32[1536,1536]{1,0:T(8,128)} custom-call(f32[10240,128]{1,0:T(8,128)S(1)} %copy-done), custom_call_target="tpu_custom_call" | custom-call | flops 9663676416 | bytes 18874368 | tf_op jit(solution)/shard_map/pallas_call | solution.py:326
  (6 shorter events, 0.1 us)
Async XLA Ops:
  0.8 5.2 %copy-start.2 = (bf16[8192,384]{1,0:T(8,128)(2,1)S(1)}, bf16[8192,384]{1,0:T(8,128)(2,1)}, u32[]{:S(2)}) copy-start(bf16[8192,384]{1,0:T(8,128)(2,1)} %param.6) | copy-start | bytes 18874372
  11.3 41.2 %all-to-all-start = ((bf16[4,1024,384]{1,2,0:T(8,128)(2,1)}), bf16[4,1024,384]{1,2,0:T(8,128)(2,1)S(1)}, u32[]{:S(2)}, u32[]{:S(2)}) async-start(bf16[4,1024,384]{1,2,0:T(8,128)(2,1)} %copy.5), calls=%async_computation | async-start | bytes 6291456 | tf_op jit(solution)/shard_map/all_to_all | solution.py:365
  20.2 37.0 %copy-start.3 = (s32[1536]{0:T(1024)S(1)}, s32[1536]{0:T(1024)}, u32[]{:S(2)}) copy-start(s32[1536]{0:T(1024)} %param.8) | copy-start | bytes 18436
  20.2 37.0 %copy-start.4 = (f32[512]{0:T(512)S(1)}, f32[512]{0:T(512)}, u32[]{:S(2)}) copy-start(f32[512]{0:T(512)} %param.9) | copy-start | bytes 6148
  52.6 41.7 %all-to-all-start.1 = ((bf16[4,1024,384]{1,2,0:T(8,128)(2,1)}), bf16[4,1024,384]{1,2,0:T(8,128)(2,1)}, u32[]{:S(2)}, u32[]{:S(2)}) async-start(bf16[4,1024,384]{1,2,0:T(8,128)(2,1)} %copy.6), calls=%async_computation.1 | async-start | bytes 6291456 | tf_op jit(solution)/shard_map/all_to_all | solution.py:365
  94.3 10.2 %copy-start.1 = (bf16[1536,1024]{1,0:T(8,128)(2,1)S(1)}, bf16[1536,1024]{1,0:T(8,128)(2,1)}, u32[]{:S(2)}) copy-start(bf16[1536,1024]{1,0:T(8,128)(2,1)} %gather_fusion) | copy-start | bytes 9437188
  199.6 2.5 copy-start

commit v4 on v3

--- a/solution.py
+++ b/solution.py
@@ -57,7 +57,7 @@
 
 TILES = [(i, j) for i in range(N // NB) for j in range(i, N // NB)]
 MESH = pl.DeviceIdType.MESH
-PIECES = 4
+PIECES = 8
 
 
 def sum_kernel(sizes, *refs):

time: 287 us -> 283 us (0.986)
  Pallas kernels: 165 us -> 161 us
    pallas_call x1, Pallas kernels: 81 us -> 76.8 us  [summed(): pl.pallas_call(functools.partial(sum_kernel, sizes), out_shape=jax.ShapeD...]
where the time goes in v4:
time: 283 us; the launch traced here: 282 us
  Pallas kernels  161 us (57%)
  waiting for transfers between devices  63.3 us (22%)
  local copies, waits for them, and re-layouts  26.2 us (9%)
  matrix products  13.3 us (5%)
  other arithmetic  9.18 us (3%)
  starting transfers between devices  8.9 us (3%)
    pallas_call x1, Pallas kernels, factor_of(): pl.pallas_call(functools.partial(cholesky_kernel, scale), out_shape=jax.S...  84.2 us
    pallas_call x1, Pallas kernels, summed(): pl.pallas_call(functools.partial(sum_kernel, sizes), out_shape=jax.ShapeD...  76.8 us
    all_to_all x2, waiting for transfers between devices, shards(): lax.all_to_all(filtered, 'gauge', split_axis=0, concat_axis=1, tiled=True)  63.3 us
    gather x2, local copies, waits for them, and re-layouts, rosette_rotate(): picked = jnp.take(full_rows, column_map, axis=1)  16.1 us
    all_to_all x2, starting transfers between devices, shards(): lax.all_to_all(filtered, 'gauge', split_axis=0, concat_axis=1, tiled=True)  8.9 us
    dot_general x8, matrix products, gram_strips(): lax.dot_general(rotated[:, at:at + TB], rotated[:, at:], (((0,), (0,)), (...  8.09 us
    all_to_all x2, local copies, waits for them, and re-layouts, shards(): lax.all_to_all(filtered, 'gauge', split_axis=0, concat_axis=1, tiled=True)  7.57 us
  transfers between devices with their start and end apart: 2, of which 2 were waited for; matrix products, arithmetic and copies ran while one was open for 4% of the time, Pallas kernels for 0%

profile of v4, /device:TPU:0, one launch (start us, length us, event | category | flops | bytes accessed | tf_op | source)
XLA Modules:
  0.0 282.1 jit_solution(3173856169005510365)
XLA Ops:
  0.0 0.8 fusion.108
  0.8 0.0 copy-start.2
  0.8 2.6 fusion.57
  3.4 2.6 fusion.60
  6.0 0.0 copy-done.2
  6.0 2.4 fusion
  8.4 2.9 %copy.5 = bf16[4,1024,384]{1,2,0:T(8,128)(2,1)} copy(bf16[4,1024,384]{2,1,0:T(8,128)(2,1)S(1)} %bitcast.22) | data formatting | bytes 6291456 | tf_op jit(solution)/shard_map/all_to_all | solution.py:365
  11.3 4.2 %all-to-all-start = ((bf16[4,1024,384]{1,2,0:T(8,128)(2,1)}), bf16[4,1024,384]{1,2,0:T(8,128)(2,1)S(1)}, u32[]{:S(2)}, u32[]{:S(2)}) async-start(bf16[4,1024,384]{1,2,0:T(8,128)(2,1)} %copy.5), calls=%async_computation | async-start | bytes 6291456 | tf_op jit(solution)/shard_map/all_to_all | solution.py:365
  15.6 4.7 %copy.6 = bf16[4,1024,384]{1,2,0:T(8,128)(2,1)} copy(bf16[4,1024,384]{2,1,0:T(8,128)(2,1)} %bitcast.21) | data formatting | bytes 6291456 | tf_op jit(solution)/shard_map/all_to_all | solution.py:365
  20.2 0.0 copy-start.3
  20.2 0.0 copy-start.4
  20.2 32.3 %all-to-all-done = bf16[4,1024,384]{1,2,0:T(8,128)(2,1)S(1)} async-done(((bf16[4,1024,384]{1,2,0:T(8,128)(2,1)}), bf16[4,1024,384]{1,2,0:T(8,128)(2,1)S(1)}, u32[]{:S(2)}, u32[]{:S(2)}) %all-to-all-start) | async-done | bytes 3145760 | tf_op jit(solution)/shard_map/all_to_all | solution.py:365
  52.6 4.7 %all-to-all-start.1 = ((bf16[4,1024,384]{1,2,0:T(8,128)(2,1)}), bf16[4,1024,384]{1,2,0:T(8,128)(2,1)}, u32[]{:S(2)}, u32[]{:S(2)}) async-start(bf16[4,1024,384]{1,2,0:T(8,128)(2,1)} %copy.6), calls=%async_computation.1 | async-start | bytes 6291456 | tf_op jit(solution)/shard_map/all_to_all | solution.py:365
  57.3 0.0 copy-done.3
  57.3 0.0 copy-done.4
  57.4 5.9 %gather_fusion = bf16[1536,1024]{1,0:T(8,128)(2,1)} fusion(bf16[1024,1536]{0,1:T(8,128)(2,1)S(1)} %bitcast.20, s32[2048]{0:T(1024)S(1)} %pad_clamp_fusion), kind=kCustom, calls=%fused_computation.clone | custom fusion | bytes 6297600 | tf_op jit(solution)/shard_map/jit(_take)/gather | solution.py:37
  63.3 31.0 %all-to-all-done.1 = bf16[4,1024,384]{1,2,0:T(8,128)(2,1)} async-done(((bf16[4,1024,384]{1,2,0:T(8,128)(2,1)}), bf16[4,1024,384]{1,2,0:T(8,128)(2,1)}, u32[]{:S(2)}, u32[]{:S(2)}) %all-to-all-start.1) | async-done | bytes 3145760 | tf_op jit(solution)/shard_map/all_to_all | solution.py:365
  94.3 0.0 copy-start.1
  94.3 10.2 %gather_fusion.1 = bf16[1536,1024]{1,0:T(8,128)(2,1)} fusion(bf16[1024,1536]{0,1:T(8,128)(2,1)} %bitcast.8, s32[2048]{0:T(1024)S(1)} %pad_clamp_fusion), kind=kCustom, calls=%fused_computation.1.clone | custom fusion | bytes 6297600 | tf_op jit(solution)/shard_map/jit(_take)/gather | solution.py:37
  104.5 0.0 copy-done.1
  104.5 2.5 select_bitcast_fusion
  107.0 1.6 fusion.34
  108.6 0.6 fusion.64
  109.2 1.2 fusion.26
  110.4 1.4 fusion.2
  111.9 1.8 fusion.43
  113.7 0.6 convolution_add_fusion.1.refs_3_
  114.3 0.8 fusion.52
  115.1 0.8 fusion.56.refs_2_
  115.9 1.4 fusion.14.refs_0_
  117.3 1.2 convolution_add_fusion.refs_1_
  118.6 76.8 %shard_map.46.refs_0_ = f32[10240,128]{1,0:T(8,128)} custom-call(f32[384,1536]{1,0:T(8,128)S(1)} %fusion.14.refs_0_, f32[384,1152]{1,0:T(8,128)S(1)} %convolution_add_fusion.refs_1_, f32[384,768]{1,0:T(8,128)S(1)} %fusion.56.refs_2_, f32[384,384]{1,0:T(8,128)S(1)} %convolution_add_fusion.1.refs_3_), custom_call_target="tpu_custom_call" | custom-call | flops 1310720 | bytes 20971520 | tf_op jit(solution)/shard_map/pallas_call | solution.py:199
  195.4 0.0 copy-start
  195.4 2.5 copy-done
  197.9 84.2 %shard_map.47 = f32[1536,1536]{1,0:T(8,128)} custom-call(f32[10240,128]{1,0:T(8,128)S(1)} %copy-done), custom_call_target="tpu_custom_call" | custom-call | flops 9663676416 | bytes 18874368 | tf_op jit(solution)/shard_map/pallas_call | solution.py:326
  (6 shorter events, 0.1 us)
Async XLA Ops:
  0.8 5.2 %copy-start.2 = (bf16[8192,384]{1,0:T(8,128)(2,1)S(1)}, bf16[8192,384]{1,0:T(8,128)(2,1)}, u32[]{:S(2)}) copy-start(bf16[8192,384]{1,0:T(8,128)(2,1)} %param.6) | copy-start | bytes 18874372
  11.3 41.2 %all-to-all-start = ((bf16[4,1024,384]{1,2,0:T(8,128)(2,1)}), bf16[4,1024,384]{1,2,0:T(8,128)(2,1)S(1)}, u32[]{:S(2)}, u32[]{:S(2)}) async-start(bf16[4,1024,384]{1,2,0:T(8,128)(2,1)} %copy.5), calls=%async_computation | async-start | bytes 6291456 | tf_op jit(solution)/shard_map/all_to_all | solution.py:365
  20.2 37.0 %copy-start.3 = (s32[1536]{0:T(1024)S(1)}, s32[1536]{0:T(1024)}, u32[]{:S(2)}) copy-start(s32[1536]{0:T(1024)} %param.8) | copy-start | bytes 18436
  20.2 37.0 %copy-start.4 = (f32[512]{0:T(512)S(1)}, f32[512]{0:T(512)}, u32[]{:S(2)}) copy-start(f32[512]{0:T(512)} %param.9) | copy-start | bytes 6148
  52.6 41.7 %all-to-all-start.1 = ((bf16[4,1024,384]{1,2,0:T(8,128)(2,1)}), bf16[4,1024,384]{1,2,0:T(8,128)(2,1)}, u32[]{:S(2)}, u32[]{:S(2)}) async-start(bf16[4,1024,384]{1,2,0:T(8,128)(2,1)} %copy.6), calls=%async_computation.1 | async-start | bytes 6291456 | tf_op jit(solution)/shard_map/all_to_all | solution.py:365
  94.3 10.2 %copy-start.1 = (bf16[1536,1024]{1,0:T(8,128)(2,1)S(1)}, bf16[1536,1024]{1,0:T(8,128)(2,1)}, u32[]{:S(2)}) copy-start(bf16[1536,1024]{1,0:T(8,128)(2,1)} %gather_fusion) | copy-start | bytes 9437188
  195.4 2.5 copy-start
